TPU v7x, 128 devices: a whole 4x4x4 slice. The times are simulated.
128 devices in a mesh: aa: 8 (over x_hi, z), ba: 16 (over x_lo, y, core).
Axes of the slice: x: 4 (x_hi: 2, x_lo: 2; x = x_hi * 2 + x_lo), y: 4, z: 4, core: 2. Of those that a mesh axis runs over, the one named last changes fastest.
Arguments:
- feats: bfloat16 [8, 64, 128, 256], P('aa', 'ba'), may hold values from -6 to 6
- conv_one: bfloat16 [3, 3, 3, 256, 256], replicated, may hold values from -0.078125 to 0.078125
- bias_one: float32 [256], replicated, may hold values from -3 to 3
- conv_two: bfloat16 [3, 3, 3, 256, 256], replicated, may hold values from -0.078125 to 0.078125
- bias_two: float32 [256], replicated, may hold values from -3 to 3
- patch_weight: bfloat16 [2, 2, 256, 128], replicated, may hold values from -0.1875 to 0.1875
- patch_bias: float32 [128], replicated, may hold values from -3 to 3
- embed_weight: bfloat16 [128, 2048], replicated, may hold values from -0.5 to 0.5
- embed_bias: float32 [2048], replicated, may hold values from -6 to 6
- norm_gain: float32 [2048], replicated, may hold values from 0.1 to 1.9
- w_query: bfloat16 [2048, 2048], P(None, 'ba'), may hold values from -2 to 2
- w_key: bfloat16 [2048, 2048], P(None, 'ba'), may hold values from -2 to 2
- w_value: bfloat16 [2048, 2048], P(None, 'ba'), may hold values from -0.125 to 0.125
- w_velocity: bfloat16 [2048, 128], P('ba'), may hold values from -0.5 to 0.5
Outputs:
- velocity: float32 [16384, 128], P(('aa', 'ba'))
All inputs are finite; a program needn't handle non-finite values.
Results may differ from a plain program's by a relative error of at most 0.035.
Values may be sent and summed in bfloat16 or wider, within the bound.
No kernel may reach another device: no remote copies, remote signals or barrier semaphores. Data moves between devices by JAX's collectives and lax.ppermute only.
A program may use at most 128 MiB of HBM per device.

v0:
```python
import functools
import math

import jax
import jax.numpy as jnp
from jax import lax
from jax.experimental import pallas as pl
from jax.experimental.pallas import tpu as pltpu
from jax.sharding import PartitionSpec as P

HEAD_DIM = 64
BF = jnp.bfloat16
F32 = jnp.float32
DEPTH = 144
TILE = 128
SAMPLE = 2
MIB = 2**20
TN = (((0,), (0,)), ((), ()))
HI = lax.Precision.HIGHEST


def gelu(x):
    return 0.5 * x * (1.0 + lax.erf(x * (1.0 / math.sqrt(2.0))))


def shifted(x, axis, by):
    count = lax.axis_size(axis)
    return lax.ppermute(x, axis, [(i, i + by) for i in range(count) if 0 <= i + by < count])


def frames_around(block):
    return shifted(block, "aa", 1), shifted(block, "aa", -1)


def rows_around(before, block, after):
    up = shifted(jnp.stack([before[-1], block[-1], after[-1]]), "ba", 1)
    down = shifted(jnp.stack([before[0], block[0], after[0]]), "ba", -1)
    return (before, block, after, up, down)


def from_peer(x, axis, bit):
    return lax.ppermute(x, axis, [(i, i ^ bit) for i in range(lax.axis_size(axis))])


def conv_taps(refs, w_ref, pad_ref, acc_ref):
    rows, width, chans = refs[1].shape
    for t in range(3):
        pad_ref[t, 0:width] = refs[3][t]
        for r in range(rows):
            pad_ref[t, (r + 1) * width : (r + 2) * width] = refs[t][r]
        pad_ref[t, (rows + 1) * width : (rows + 2) * width] = refs[4][t]
    for w in range(3):
        total = None
        for t in range(3):
            for r in range(3):
                part = jnp.dot(
                    pad_ref[t, r * width : (r + rows) * width],
                    w_ref[t, r, w],
                    preferred_element_type=F32,
                )
                total = part if total is None else total + part
        acc_ref[w] = total


def conv_sum(acc_ref, bias_ref, width):
    count = acc_ref.shape[1]
    at = lax.broadcasted_iota(jnp.int32, (count, 1), 0) % width
    left = jnp.where(at == 0, 0.0, pltpu.roll(acc_ref[0], 1, 0))
    right = jnp.where(at == width - 1, 0.0, pltpu.roll(acc_ref[2], count - 1, 0))
    return left + acc_ref[1] + right + bias_ref[...]


def first_kernel(*refs):
    halo, (w_ref, bias_ref, out_ref, pad_ref, acc_ref) = refs[:5], refs[5:]
    conv_taps(halo, w_ref, pad_ref, acc_ref)

    rows, width, chans = out_ref.shape
    out_ref[...] = gelu(conv_sum(acc_ref, bias_ref, width)).astype(BF).reshape(rows, width, chans)


def second_kernel(*refs):
    halo, rest = refs[:5], refs[5:]
    w_ref, bias_ref, pw_ref, pb_ref, gram_ref, keys_ref, pad_ref, acc_ref = rest
    conv_taps(halo, w_ref, pad_ref, acc_ref)

    rows, width, chans = halo[1].shape
    half = width // 2
    first = halo[1][...].reshape(rows * width, chans).astype(F32)
    second = (first + gelu(conv_sum(acc_ref, bias_ref, width))).astype(BF)
    r = lax.broadcasted_iota(jnp.int32, (width, width), 0)
    c = lax.broadcasted_iota(jnp.int32, (width, width), 1)
    picks = (c == jnp.where(r < half, 2 * r, 2 * r - (width - 1))).astype(BF)
    latents = []
    for e in range(rows // 2):
        total = pb_ref[...] + jnp.zeros((half, pb_ref.shape[1]), F32)
        for a in range(2):
            at = (2 * e + a) * width
            sorted_row = jnp.dot(
                picks, second[at : at + width], preferred_element_type=F32
            ).astype(BF)
            for k in range(2):
                total += jnp.dot(
                    sorted_row[k * half : (k + 1) * half],
                    pw_ref[a, k],
                    preferred_element_type=F32,
                )
        latents.append(total.astype(BF).astype(F32))
    latents = jnp.concatenate(latents, axis=0).T
    at = lax.broadcasted_iota(jnp.int32, (DEPTH - TILE, TILE), 0)
    columns = jnp.concatenate([latents, jnp.where(at == 0, 1.0, 0.0)], axis=0)
    spread = jnp.dot(gram_ref[...], columns, precision=HI, preferred_element_type=F32)
    spread = (spread * columns).sum(0, keepdims=True)
    rstd = lax.rsqrt(jnp.maximum(spread, 0.0) + 1e-05)
    keys = (columns * rstd).astype(BF)
    tail = jnp.where(at == 0, rstd, jnp.where(at == 1, 1.0, 0.0)).astype(BF)
    for i in range(keys_ref.shape[0]):
        keys_ref[i, 0:TILE] = keys[0:TILE]
        keys_ref[i, TILE:DEPTH] = tail


def conv_call(kernel, halo, weight, extras, out_shapes):
    rows, width, chans = halo[1].shape
    whole = [pl.BlockSpec(memory_space=pltpu.VMEM)]
    return pl.pallas_call(
        kernel,
        in_specs=whole * (len(halo) + 1 + len(extras)),
        out_specs=whole * len(out_shapes),
        out_shape=[jax.ShapeDtypeStruct(*shape) for shape in out_shapes],
        scratch_shapes=[
            pltpu.VMEM((3, (rows + 2) * width, chans), BF),
            pltpu.VMEM((3, rows * width, chans), F32),
        ],
        compiler_params=pltpu.CompilerParams(vmem_limit_bytes=32 * MIB),
        cost_estimate=pl.CostEstimate(
            flops=2 * 27 * rows * width * chans * chans,
            bytes_accessed=2 * 27 * chans * chans,
            transcendentals=0,
        ),
    )(*halo, weight, *extras)


def side(tiles):
    return jnp.concatenate(tiles, axis=1)


def chosen(even, even_ref, odd_ref, h):
    return jnp.where(even, even_ref[h].astype(F32), odd_ref[h].astype(F32)).astype(BF)


def attend_kernel(n_blocks, start, finish, heads, *refs):
    even = pl.program_id(0) % 2 == 0
    if start:
        even_ref, odd_ref, place_ref, *rest = refs
    elif finish:
        q_ref, even_ref, odd_ref, *rest = refs
    else:
        q_ref, *rest = refs
    blocks, rest = rest[:n_blocks], rest[n_blocks:]
    if not start:
        (m_in, o_in, *rest) = rest
    if finish:
        n_all = len(rest) - 4
        earlier, (own_ref, other_ref, held, sem) = rest[:n_all], rest[n_all:]
    elif start:
        q_out, m_out, out_ref = rest
    else:
        m_out, out_ref = rest

    if start:
        tile = blocks[0][place_ref[pl.program_id(0) // 2]]
        query = []
        for h in range(heads):
            form = chosen(even, even_ref.at[:, :, TILE:], odd_ref.at[:, :, TILE:], h)
            query.append(jnp.dot(form, tile, preferred_element_type=F32).astype(BF))
            q_out[h] = query[h]
        query = side(query)
    else:
        query = side([q_ref[h] for h in range(heads)])

    def scores(tiles):
        return lax.dot_general(tiles, query, TN, preferred_element_type=F32)

    if start:
        sample = side([blocks[0][i] for i in range(SAMPLE)])
        shift = scores(sample).max(0, keepdims=True)
        total = jnp.zeros((DEPTH, heads * TILE), F32)
    else:
        shift = m_in[...]
        total = side([o_in[h] for h in range(heads)])
    for block in blocks:
        keys = side([block[i] for i in range(block.shape[0])])
        probs = jnp.exp2(scores(keys) - shift).astype(BF)
        total = total + jnp.dot(keys, probs, preferred_element_type=F32)
    if not finish:
        m_out[...] = shift
        for h in range(heads):
            out_ref[h] = total[:, h * TILE : (h + 1) * TILE]
        return

    @pl.when(pl.program_id(0) == 0)
    def _():
        own_ref[...] = jnp.zeros_like(own_ref)
        other_ref[...] = jnp.zeros_like(other_ref)

    def deliver(sums):
        scaled = (sums / sums[TILE + 1 : TILE + 2]).astype(BF)
        moved = jnp.zeros((TILE, TILE), F32)
        for h in range(heads):
            moved += lax.dot_general(
                scaled[:, h * TILE : (h + 1) * TILE],
                chosen(even, even_ref, odd_ref, h),
                TN,
                preferred_element_type=F32,
            )

        @pl.when(pl.program_id(0) < 2)
        def _():
            own_ref[...] += moved

        @pl.when(pl.program_id(0) >= 2)
        def _():
            other_ref[...] += moved

    largest = jnp.where(total[TILE + 1 : TILE + 2] < 2.0**100, 0.0, 1.0).max()

    @pl.when(largest < 0.5)
    def _():
        deliver(total)

    @pl.when(largest > 0.5)
    def _():
        state = (
            jnp.full((1, heads * TILE), -1e38, F32),
            jnp.zeros((DEPTH, heads * TILE), F32),
        )

        def over(ref, state):
            def one_tile(i, state):
                best, sums = state
                keys = ref[i]
                s = scores(keys)
                peak = jnp.maximum(best, s.max(0, keepdims=True))
                probs = jnp.exp2(s - peak).astype(BF)
                sums = sums * jnp.exp2(best - peak) + jnp.dot(
                    keys, probs, preferred_element_type=F32
                )
                return peak, sums

            return lax.fori_loop(0, ref.shape[0], one_tile, state)

        for source in earlier:
            copy = pltpu.make_async_copy(source, held, sem)
            copy.start()
            copy.wait()
            state = over(held, state)
        for block in blocks:
            state = over(block, state)
        deliver(state[1])


def attend_call(sources, blocks, state, earlier=None):
    start, finish = state is None, earlier is not None
    heads = sources[0].shape[0] if start else sources[1].shape[0] if finish else 8
    n_heads = 4 * heads
    steps = 4
    per_q = pl.BlockSpec((heads, DEPTH, TILE), lambda i: (i, 0, 0))
    per_m = pl.BlockSpec((1, heads * TILE), lambda i: (0, i))
    whole = pl.BlockSpec(memory_space=pltpu.VMEM)
    args = [*sources, *blocks]
    if start:
        specs = [whole] * 2 + [pl.BlockSpec(memory_space=pltpu.SMEM)]
    elif finish:
        specs = [per_q] + [pl.BlockSpec((heads, DEPTH, TILE), lambda i: (0, 0, 0))] * 2
    else:
        specs = [per_q]
    specs = specs + [whole] * len(blocks)
    if not start:
        args += list(state)
        specs += [per_m, per_q]
    shape = (n_heads, DEPTH, TILE)
    scratch = []
    if finish:
        args += earlier
        specs += [pl.BlockSpec(memory_space=pl.ANY)] * len(earlier)
        out_specs = [whole] * 2
        out_shape = [jax.ShapeDtypeStruct((TILE, TILE), F32)] * 2
        scratch = [pltpu.VMEM(blocks[0].shape, BF), pltpu.SemaphoreType.DMA(())]
    else:
        out_specs = [per_m, per_q]
        out_shape = [
            jax.ShapeDtypeStruct((1, n_heads * TILE), F32),
            jax.ShapeDtypeStruct(shape, F32),
        ]
        if start:
            out_specs = [per_q] + out_specs
            out_shape = [jax.ShapeDtypeStruct(shape, BF)] + out_shape
    pairs = steps * heads * TILE * sum(b.shape[0] for b in blocks) * TILE
    return pl.pallas_call(
        functools.partial(attend_kernel, len(blocks), start, finish, heads),
        grid=(steps,),
        in_specs=specs,
        out_specs=out_specs,
        out_shape=out_shape,
        scratch_shapes=scratch,
        compiler_params=pltpu.CompilerParams(vmem_limit_bytes=44 * MIB),
        cost_estimate=pl.CostEstimate(
            flops=pairs * 1024, bytes_accessed=4 * MIB, transcendentals=pairs
        ),
    )(*args)


def projections(embed_weight, embed_bias, norm_gain, w_query, w_key, w_value, w_velocity):
    width = w_query.shape[1]
    heads = width // HEAD_DIM
    latent, features = embed_weight.shape
    embed = jnp.concatenate(
        [
            embed_weight.astype(F32),
            embed_bias[None],
            jnp.zeros((DEPTH - latent - 1, features), F32),
        ],
        axis=0,
    )
    embed = embed - embed.mean(1, keepdims=True)
    gram = lax.dot_general(embed, embed, (((1,), (1,)), ((), ())), precision=HI) / features
    gained = embed * norm_gain
    high = gained.astype(BF)
    low = (gained - high.astype(F32)).astype(BF)
    joined = jnp.dot(
        jnp.concatenate([high, low], axis=0),
        jnp.concatenate([w_query, w_key, w_value], axis=1),
        preferred_element_type=F32,
    )
    joined = (joined[:DEPTH] + joined[DEPTH:]).reshape(DEPTH, 3, heads, HEAD_DIM)
    scale = HEAD_DIM ** (-0.5) * math.log2(math.e)
    forms = jnp.einsum("ehf,dhf->hed", joined[:, 1], joined[:, 0] * scale, precision=HI)
    outs = jnp.einsum(
        "ehf,hfc->hec",
        joined[:, 2],
        w_velocity.astype(F32).reshape(heads, HEAD_DIM, -1),
        precision=HI,
    )
    return gram, jnp.concatenate([outs, forms], axis=-1).astype(BF)


def on_device(
    feats,
    conv_one,
    bias_one,
    conv_two,
    bias_two,
    patch_weight,
    patch_bias,
    embed_weight,
    embed_bias,
    norm_gain,
    w_query,
    w_key,
    w_value,
    w_velocity,
):
    rows, width, chans = feats.shape[1:]
    gram, maps = projections(
        embed_weight, embed_bias, norm_gain, w_query, w_key, w_value, w_velocity
    )
    peers = lax.axis_size("ba")
    bits = [peers >> k for k in range(1, peers.bit_length())]

    block = feats[0]
    before, after, maps = lax.optimization_barrier((*frames_around(block), maps))
    halo = rows_around(before, block, after)
    others = from_peer(maps, "ba", bits[0])
    for bit in bits[1:-1]:
        maps = jnp.concatenate([maps, others], axis=0)
        others = from_peer(maps, "ba", bit)
    maps = [maps, others]
    (first,) = conv_call(
        first_kernel, halo, conv_one, [bias_one[None]], [((rows, width, chans), BF)]
    )
    before, after = frames_around(first)
    halo = rows_around(before, first, after)
    tokens = rows * width // 4
    (keys,) = conv_call(
        second_kernel,
        halo,
        conv_two,
        [bias_two[None], patch_weight, patch_bias[None], gram],
        [((peers, DEPTH, tokens), BF)],
    )
    block = lax.all_to_all(keys, "ba", 0, 0, tiled=True)
    count = lax.axis_size("aa")
    inner = count // 2
    def send(source, dx, dz):
        pairs = [
            (x * inner + z, (x + dx) % 2 * inner + (z + dz) % inner)
            for x in range(2)
            for z in range(inner)
        ]
        return lax.ppermute(source, "aa", pairs)

    near = [send(block, 0, 1), send(block, 0, 3), send(block, 1, 0)]

    me = lax.axis_index("ba")
    places = jnp.stack([me, me ^ 1]).astype(jnp.int32)
    queries, *state = attend_call([*maps, places], [block], None)
    block, near, state = lax.optimization_barrier((block, near, state))
    far = [
        send(block, 1, 2),
        send(near[0], 0, 1),
        send(near[0], 1, 0),
        send(near[2], 0, 3),
    ]
    state = attend_call([queries], near, state)
    earlier = [block, *near]
    own, theirs = attend_call([queries, *maps], far, state, earlier)
    return own + from_peer(theirs, "ba", bits[-1])


def solution(mesh):
    return jax.shard_map(
        on_device,
        mesh=mesh,
        in_specs=(
            P("aa", "ba", None, None),
            P(),
            P(),
            P(),
            P(),
            P(),
            P(),
            P(),
            P(),
            P(),
            P(None, "ba"),
            P(None, "ba"),
            P(None, "ba"),
            P("ba", None),
        ),
        out_specs=P(("aa", "ba"), None),
        check_vma=False,
    )
```

profile of v0, /device:TPU:1, one launch (start us, length us, event | category | flops | bytes accessed | tf_op | source)
XLA Modules:
  0.0 171.2 jit_solution(15020190229465538565)
XLA Ops:
  0.0 1.4 collective-permute-start.1
  1.4 5.0 %collective-permute-start = (bf16[4,128,256]{2,1,0:T(8,128)(2,1)}, bf16[4,128,256]{2,1,0:T(8,128)(2,1)S(1)}, u32[]{:S(2)}, u32[]{:S(2)}) collective-permute-start(bf16[4,128,256]{2,1,0:T(8,128)(2,1)} %bitcast.25), channel_id=1, source_target_pairs={{0,16},{16,32},{32,48},{48,64},{64,80},{80,96},{96,112},{1,17},{17... | collective-permute-start | bytes 786440 | tf_op jit(solution)/shard_map/ppermute | solution.py:28
  6.5 1.1 convert_element_type.14
  11.8 4.9 %collective-permute-start.5 = (bf16[3,128,256]{2,1,0:T(8,128)(2,1)S(1)}, bf16[3,128,256]{2,1,0:T(8,128)(2,1)S(1)}, u32[]{:S(2)}, u32[]{:S(2)}) collective-permute-start(bf16[3,128,256]{2,1,0:T(8,128)(2,1)S(1)} %pad_maximum_fusion.2), channel_id=1, source_target_pairs={{0,1},{1,2},{2,3},{3,4},{4,5},{5,6},{6,7},{7,8},{8,9},{9,10},{10,1... | collective-permute-start | bytes 589832 | tf_op jit(solution)/shard_map/ppermute | solution.py:28
  16.7 1.9 %collective-permute-start.6 = (bf16[3,128,256]{2,1,0:T(8,128)(2,1)S(1)}, bf16[3,128,256]{2,1,0:T(8,128)(2,1)S(1)}, u32[]{:S(2)}, u32[]{:S(2)}) collective-permute-start(bf16[3,128,256]{2,1,0:T(8,128)(2,1)S(1)} %pad_maximum_fusion.3), channel_id=1, source_target_pairs={{1,0},{2,1},{3,2},{4,3},{5,4},{6,5},{7,6},{8,7},{9,8},{10,9},{11,1... | collective-permute-start | bytes 589832 | tf_op jit(solution)/shard_map/ppermute | solution.py:28
  18.7 1.3 convolution_multiply_fusion.refs_9_
  20.0 1.3 collective-permute-start.2
  21.3 2.4 %collective-permute-done.6.refs_4_ = bf16[3,128,256]{2,1,0:T(8,128)(2,1)S(1)} collective-permute-done((bf16[3,128,256]{2,1,0:T(8,128)(2,1)S(1)}, bf16[3,128,256]{2,1,0:T(8,128)(2,1)S(1)}, u32[]{:S(2)}, u32[]{:S(2)}) %collective-permute-start.6) | collective-permute-done | bytes 196640 | tf_op jit(solution)/shard_map/ppermute | solution.py:28
  23.7 2.0 %shard_map.136.refs_1_ = bf16[4,128,256]{2,1,0:T(8,128)(2,1)S(1)} custom-call(bf16[4,128,256]{2,1,0:T(8,128)(2,1)S(1)} %collective-permute-done.refs_0_, bf16[4,128,256]{2,1,0:T(8,128)(2,1)S(1)} %bitcast.26, bf16[4,128,256]{2,1,0:T(8,128)(2,1)S(1)} %collective-permute-done.1.refs_2_, bf16[3,128,256]{2,1,0:T(8,128)(2,1)S(1)} %collective-permute-done.5.refs_3_, ...), custom_call_target="tpu_custom_call" | custom-call | flops 1811939328 | bytes 3538944 | tf_op jit(solution)/shard_map/pallas_call | solution.py:124
  25.8 1.3 collective-permute-start.8
  27.2 2.7 %collective-permute-start.3 = (bf16[4,144,272]{2,1,0:T(8,128)(2,1)S(1)}, bf16[4,144,272]{2,1,0:T(8,128)(2,1)S(1)}, u32[]{:S(2)}, u32[]{:S(2)}) collective-permute-start(bf16[4,144,272]{2,1,0:T(8,128)(2,1)S(1)} %pad_maximum_fusion), channel_id=1, source_target_pairs={{0,4},{1,5},{2,6},{3,7},{4,0},{5,1},{6,2},{7,3},{8,12},{9,13},{10,... | collective-permute-start | bytes 940040 | tf_op jit(solution)/shard_map/ppermute | solution.py:42
  29.9 4.6 %collective-permute-start.7 = (bf16[4,128,256]{2,1,0:T(8,128)(2,1)S(1)}, bf16[4,128,256]{2,1,0:T(8,128)(2,1)S(1)}, u32[]{:S(2)}, u32[]{:S(2)}) collective-permute-start(bf16[4,128,256]{2,1,0:T(8,128)(2,1)S(1)} %shard_map.136.refs_1_), channel_id=1, source_target_pairs={{0,16},{16,32},{32,48},{48,64},{64,80},{80,96},{96,112},{1,17},{17... | collective-permute-start | bytes 786440 | tf_op jit(solution)/shard_map/ppermute | solution.py:28
  34.6 1.4 collective-permute-done.8.refs_2_
  36.0 3.6 %collective-permute-done.7.refs_0_ = bf16[4,128,256]{2,1,0:T(8,128)(2,1)S(1)} collective-permute-done((bf16[4,128,256]{2,1,0:T(8,128)(2,1)S(1)}, bf16[4,128,256]{2,1,0:T(8,128)(2,1)S(1)}, u32[]{:S(2)}, u32[]{:S(2)}) %collective-permute-start.7) | collective-permute-done | bytes 262176 | tf_op jit(solution)/shard_map/ppermute | solution.py:28
  39.6 1.9 %collective-permute-start.9 = (bf16[3,128,256]{2,1,0:T(8,128)(2,1)S(1)}, bf16[3,128,256]{2,1,0:T(8,128)(2,1)S(1)}, u32[]{:S(2)}, u32[]{:S(2)}) collective-permute-start(bf16[3,128,256]{2,1,0:T(8,128)(2,1)S(1)} %pad_maximum_fusion.4), channel_id=1, source_target_pairs={{0,1},{1,2},{2,3},{3,4},{4,5},{5,6},{6,7},{7,8},{8,9},{9,10},{10,1... | collective-permute-start | bytes 589832 | tf_op jit(solution)/shard_map/ppermute | solution.py:28
  41.6 2.7 %collective-permute-start.10 = (bf16[3,128,256]{2,1,0:T(8,128)(2,1)S(1)}, bf16[3,128,256]{2,1,0:T(8,128)(2,1)S(1)}, u32[]{:S(2)}, u32[]{:S(2)}) collective-permute-start(bf16[3,128,256]{2,1,0:T(8,128)(2,1)S(1)} %pad_maximum_fusion.5), channel_id=1, source_target_pairs={{1,0},{2,1},{3,2},{4,3},{5,4},{6,5},{7,6},{8,7},{9,8},{10,9},{11,1... | collective-permute-start | bytes 589832 | tf_op jit(solution)/shard_map/ppermute | solution.py:28
  44.5 2.0 %collective-permute-start.4 = (bf16[8,144,272]{2,1,0:T(8,128)(2,1)S(1)}, bf16[8,144,272]{2,1,0:T(8,128)(2,1)S(1)}, u32[]{:S(2)}, u32[]{:S(2)}) collective-permute-start(bf16[8,144,272]{2,1,0:T(8,128)(2,1)S(1)} %constant_dynamic-update-slice_fusion.refs_0_.refs_1_), channel_id=1, source_target_pairs={{0,2},{1,3},{2,0},{3,1},{4,6},{5,7},{6,4},{7,5},{8,10},{9,11},{10,... | collective-permute-start | bytes 1880072 | tf_op jit(solution)/shard_map/ppermute | solution.py:42
  46.4 5.1 %collective-permute-done.10.refs_4_ = bf16[3,128,256]{2,1,0:T(8,128)(2,1)S(1)} collective-permute-done((bf16[3,128,256]{2,1,0:T(8,128)(2,1)S(1)}, bf16[3,128,256]{2,1,0:T(8,128)(2,1)S(1)}, u32[]{:S(2)}, u32[]{:S(2)}) %collective-permute-start.10) | collective-permute-done | bytes 196640 | tf_op jit(solution)/shard_map/ppermute | solution.py:28
  51.5 4.3 %shard_map.137 = bf16[16,144,128]{2,1,0:T(8,128)(2,1)} custom-call(bf16[4,128,256]{2,1,0:T(8,128)(2,1)S(1)} %collective-permute-done.7.refs_0_, bf16[4,128,256]{2,1,0:T(8,128)(2,1)S(1)} %shard_map.136.refs_1_, bf16[4,128,256]{2,1,0:T(8,128)(2,1)S(1)} %collective-permute-done.8.refs_2_, bf16[3,128,256]{2,1,0:T(8,128)(2,1)S(1)} %collective-permute-done.9.refs_3_, ...), custom_call_target="tpu_custom_call" | custom-call | flops 1811939328 | bytes 3538944 | tf_op jit(solution)/shard_map/pallas_call | solution.py:124
  55.8 5.8 %all-to-all-start = ((bf16[16,144,128]{2,1,0:T(8,128)(2,1)}), bf16[16,144,128]{2,1,0:T(8,128)(2,1)S(1)}, u32[]{:S(2)}, u32[]{:S(2)}) async-start(bf16[16,144,128]{2,1,0:T(8,128)(2,1)} %shard_map.137), calls=%async_computation | async-start | bytes 1179648 | tf_op jit(solution)/shard_map/all_to_all | solution.py:390
  61.6 13.4 %all-to-all-done.refs_3_.refs_9_ = bf16[16,144,128]{2,1,0:T(8,128)(2,1)S(1)} async-done(((bf16[16,144,128]{2,1,0:T(8,128)(2,1)}), bf16[16,144,128]{2,1,0:T(8,128)(2,1)S(1)}, u32[]{:S(2)}, u32[]{:S(2)}) %all-to-all-start) | async-done | bytes 589856 | tf_op jit(solution)/shard_map/all_to_all | solution.py:390
  75.0 15.1 %collective-permute-start.13 = (bf16[16,144,128]{2,1,0:T(8,128)(2,1)S(1)}, bf16[16,144,128]{2,1,0:T(8,128)(2,1)S(1)}, u32[]{:S(2)}, u32[]{:S(2)}) collective-permute-start(bf16[16,144,128]{2,1,0:T(8,128)(2,1)S(1)} %all-to-all-done.refs_3_.refs_9_), channel_id=1, source_target_pairs={{0,64},{16,80},{32,96},{48,112},{64,0},{80,16},{96,32},{112,48},{1... | collective-permute-start | bytes 1769480 | tf_op jit(solution)/shard_map/ppermute | solution.py:399
  90.2 1.5 collective-permute-start.11
  91.6 9.6 %shard_map.138 = (bf16[32,144,128]{2,1,0:T(8,128)(2,1)S(1)}, f32[1,4096]{1,0:T(1,128)S(1)}, f32[32,144,128]{2,1,0:T(8,128)S(1)}) custom-call(bf16[8,144,272]{2,1,0:T(8,128)(2,1)S(1)} %constant_dynamic-update-slice_fusion.refs_0_.refs_1_, bf16[8,144,272]{2,1,0:T(8,128)(2,1)S(1)} %collective-permute-done.4.refs_1_.refs_2_, s32[2]{0:T(128)S(1)} %pad_add_fusion.refs_2_, ...), custom_call_target="tpu_custom_call" | custom-call | flops 8589934592 | bytes 4194304 | tf_op jit(solution)/shard_map/pallas_call | solution.py:298
  101.2 2.3 %collective-permute-done.13.refs_3_.refs_12_ = bf16[16,144,128]{2,1,0:T(8,128)(2,1)S(1)} collective-permute-done((bf16[16,144,128]{2,1,0:T(8,128)(2,1)S(1)}, bf16[16,144,128]{2,1,0:T(8,128)(2,1)S(1)}, u32[]{:S(2)}, u32[]{:S(2)}) %collective-permute-start.13) | collective-permute-done | bytes 589856 | tf_op jit(solution)/shard_map/ppermute | solution.py:399
  104.3 1.2 collective-permute-done.11.refs_1_.refs_10_
  106.2 3.6 %collective-permute-start.14 = (bf16[16,144,128]{2,1,0:T(8,128)(2,1)S(1)}, bf16[16,144,128]{2,1,0:T(8,128)(2,1)S(1)}, u32[]{:S(2)}, u32[]{:S(2)}) collective-permute-start(bf16[16,144,128]{2,1,0:T(8,128)(2,1)S(1)} %all-to-all-done.refs_3_.refs_9_), channel_id=1, source_target_pairs={{0,96},{16,112},{32,64},{48,80},{64,32},{80,48},{96,0},{112,16},{1... | collective-permute-start | bytes 1769480 | tf_op jit(solution)/shard_map/ppermute | solution.py:399
  109.8 1.1 collective-permute-start.17
  110.9 22.0 %shard_map.139 = (f32[1,4096]{1,0:T(1,128)S(1)}, f32[32,144,128]{2,1,0:T(8,128)S(1)}) custom-call(bf16[32,144,128]{2,1,0:T(8,128)(2,1)S(1)} %get-tuple-element.24.refs_0_, bf16[16,144,128]{2,1,0:T(8,128)(2,1)S(1)} %collective-permute-done.11.refs_1_.refs_10_, bf16[16,144,128]{2,1,0:T(8,128)(2,1)S(1)} %collective-permute-done.12.refs_2_.refs_11_, ...), custom_call_target="tpu_custom_call" | custom-call | flops 25769803776 | bytes 4194304 | tf_op jit(solution)/shard_map/pallas_call | solution.py:298
  133.3 2.1 %collective-permute-done.17.refs_6_ = bf16[16,144,128]{2,1,0:T(8,128)(2,1)S(1)} collective-permute-done((bf16[16,144,128]{2,1,0:T(8,128)(2,1)S(1)}, bf16[16,144,128]{2,1,0:T(8,128)(2,1)S(1)}, u32[]{:S(2)}, u32[]{:S(2)}) %collective-permute-start.17) | collective-permute-done | bytes 589856 | tf_op jit(solution)/shard_map/ppermute | solution.py:399
  135.4 31.2 %shard_map.140 = (f32[128,128]{1,0:T(8,128)S(1)}, f32[128,128]{1,0:T(8,128)S(1)}) custom-call(bf16[32,144,128]{2,1,0:T(8,128)(2,1)S(1)} %get-tuple-element.24.refs_0_, bf16[8,144,272]{2,1,0:T(8,128)(2,1)S(1)} %constant_dynamic-update-slice_fusion.refs_0_.refs_1_, bf16[8,144,272]{2,1,0:T(8,128)(2,1)S(1)} %collective-permute-done.4.refs_1_.refs_2_, ...), custom_call_target="tpu_custom_call" | custom-call | flops 34359738368 | bytes 4194304 | tf_op jit(solution)/shard_map/pallas_call | solution.py:298
  166.6 3.1 %collective-permute-start.18 = (f32[128,128]{1,0:T(8,128)S(1)}, f32[128,128]{1,0:T(8,128)S(1)}, u32[]{:S(2)}, u32[]{:S(2)}) collective-permute-start(f32[128,128]{1,0:T(8,128)S(1)} %get-tuple-element.36), channel_id=1, source_target_pairs={{0,1},{1,0},{2,3},{3,2},{4,5},{5,4},{6,7},{7,6},{8,9},{9,8},{10,11... | collective-permute-start | bytes 196616 | tf_op jit(solution)/shard_map/ppermute | solution.py:42
  (67 shorter events, 7.8 us)
Async XLA Ops:
  0.0 10.8 %copy-start = (bf16[128,128]{1,0:T(8,128)(2,1)S(1)}, bf16[128,128]{1,0:T(8,128)(2,1)}, u32[]{:S(2)}) copy-start(bf16[128,128]{1,0:T(8,128)(2,1)} %param.27) | copy-start | bytes 98308
  0.0 7.7 %copy-start.8 = (f32[2048]{0:T(1024)S(1)}, f32[2048]{0:T(1024)}, u32[]{:S(2)}) copy-start(f32[2048]{0:T(1024)} %param.22) | copy-start | bytes 24580
  0.0 8.0 %copy-start.9 = (f32[2048]{0:T(1024)S(1)}, f32[2048]{0:T(1024)}, u32[]{:S(2)}) copy-start(f32[2048]{0:T(1024)} %param.23) | copy-start | bytes 24580
  0.0 11.2 %collective-permute-start.1 = (bf16[4,128,256]{2,1,0:T(8,128)(2,1)}, bf16[4,128,256]{2,1,0:T(8,128)(2,1)S(1)}, u32[]{:S(2)}, u32[]{:S(2)}) collective-permute-start(bf16[4,128,256]{2,1,0:T(8,128)(2,1)} %bitcast.24), channel_id=1, source_target_pairs={{16,0},{32,16},{48,32},{64,48},{80,64},{96,80},{112,96},{17,1},{33... | collective-permute-start | bytes 786440 | tf_op jit(solution)/shard_map/ppermute | solution.py:28
  1.4 10.3 %collective-permute-start = (bf16[4,128,256]{2,1,0:T(8,128)(2,1)}, bf16[4,128,256]{2,1,0:T(8,128)(2,1)S(1)}, u32[]{:S(2)}, u32[]{:S(2)}) collective-permute-start(bf16[4,128,256]{2,1,0:T(8,128)(2,1)} %bitcast.25), channel_id=1, source_target_pairs={{0,16},{16,32},{32,48},{48,64},{64,80},{80,96},{96,112},{1,17},{17... | collective-permute-start | bytes 786440 | tf_op jit(solution)/shard_map/ppermute | solution.py:28
  7.9 1.2 copy-start.11
  8.0 1.3 copy-start.12
  10.1 1.1 copy-start.1
  11.7 12.0 %copy-start.2 = (bf16[3,3,3,256,256]{4,3,2,1,0:T(8,128)(2,1)S(1)}, bf16[3,3,3,256,256]{4,3,2,1,0:T(8,128)(2,1)}, u32[]{:S(2)}) copy-start(bf16[3,3,3,256,256]{4,3,2,1,0:T(8,128)(2,1)} %refs_5_.2) | copy-start | bytes 10616836
  11.8 9.5 %collective-permute-start.5 = (bf16[3,128,256]{2,1,0:T(8,128)(2,1)S(1)}, bf16[3,128,256]{2,1,0:T(8,128)(2,1)S(1)}, u32[]{:S(2)}, u32[]{:S(2)}) collective-permute-start(bf16[3,128,256]{2,1,0:T(8,128)(2,1)S(1)} %pad_maximum_fusion.2), channel_id=1, source_target_pairs={{0,1},{1,2},{2,3},{3,4},{4,5},{5,6},{6,7},{7,8},{8,9},{9,10},{10,1... | collective-permute-start | bytes 589832 | tf_op jit(solution)/shard_map/ppermute | solution.py:28
  16.7 7.0 %copy-start.5 = (f32[256]{0:T(256)S(1)}, f32[256]{0:T(256)}, u32[]{:S(2)}) copy-start(f32[256]{0:T(256)} %param.16) | copy-start | bytes 3076
  16.7 7.0 %collective-permute-start.6 = (bf16[3,128,256]{2,1,0:T(8,128)(2,1)S(1)}, bf16[3,128,256]{2,1,0:T(8,128)(2,1)S(1)}, u32[]{:S(2)}, u32[]{:S(2)}) collective-permute-start(bf16[3,128,256]{2,1,0:T(8,128)(2,1)S(1)} %pad_maximum_fusion.3), channel_id=1, source_target_pairs={{1,0},{2,1},{3,2},{4,3},{5,4},{6,5},{7,6},{8,7},{9,8},{10,9},{11,1... | collective-permute-start | bytes 589832 | tf_op jit(solution)/shard_map/ppermute | solution.py:28
  20.0 7.1 %collective-permute-start.2 = (bf16[2,144,272]{2,1,0:T(8,128)(2,1)S(1)}, bf16[2,144,272]{2,1,0:T(8,128)(2,1)S(1)}, u32[]{:S(2)}, u32[]{:S(2)}) collective-permute-start(bf16[2,144,272]{2,1,0:T(8,128)(2,1)S(1)} %pad_maximum_fusion.1), channel_id=1, source_target_pairs={{0,8},{1,9},{2,10},{3,11},{4,12},{5,13},{6,14},{7,15},{8,0},{9,1},... | collective-permute-start | bytes 470024 | tf_op jit(solution)/shard_map/ppermute | solution.py:42
  23.7 27.8 %copy-start.4 = (bf16[2,2,256,128]{3,2,1,0:T(8,128)(2,1)S(1)}, bf16[2,2,256,128]{3,2,1,0:T(8,128)(2,1)}, u32[]{:S(2)}) copy-start(bf16[2,2,256,128]{3,2,1,0:T(8,128)(2,1)} %refs_7_.1) | copy-start | bytes 786436
  25.8 10.2 %collective-permute-start.8 = (bf16[4,128,256]{2,1,0:T(8,128)(2,1)S(1)}, bf16[4,128,256]{2,1,0:T(8,128)(2,1)S(1)}, u32[]{:S(2)}, u32[]{:S(2)}) collective-permute-start(bf16[4,128,256]{2,1,0:T(8,128)(2,1)S(1)} %shard_map.136.refs_1_), channel_id=1, source_target_pairs={{16,0},{32,16},{48,32},{64,48},{80,64},{96,80},{112,96},{17,1},{33... | collective-permute-start | bytes 786440 | tf_op jit(solution)/shard_map/ppermute | solution.py:28
  27.1 24.4 %copy-start.3 = (bf16[3,3,3,256,256]{4,3,2,1,0:T(8,128)(2,1)S(1)}, bf16[3,3,3,256,256]{4,3,2,1,0:T(8,128)(2,1)}, u32[]{:S(2)}) copy-start(bf16[3,3,3,256,256]{4,3,2,1,0:T(8,128)(2,1)} %refs_5_.3) | copy-start | bytes 10616836
  27.2 17.2 %collective-permute-start.3 = (bf16[4,144,272]{2,1,0:T(8,128)(2,1)S(1)}, bf16[4,144,272]{2,1,0:T(8,128)(2,1)S(1)}, u32[]{:S(2)}, u32[]{:S(2)}) collective-permute-start(bf16[4,144,272]{2,1,0:T(8,128)(2,1)S(1)} %pad_maximum_fusion), channel_id=1, source_target_pairs={{0,4},{1,5},{2,6},{3,7},{4,0},{5,1},{6,2},{7,3},{8,12},{9,13},{10,... | collective-permute-start | bytes 940040 | tf_op jit(solution)/shard_map/ppermute | solution.py:42
  29.9 9.7 %collective-permute-start.7 = (bf16[4,128,256]{2,1,0:T(8,128)(2,1)S(1)}, bf16[4,128,256]{2,1,0:T(8,128)(2,1)S(1)}, u32[]{:S(2)}, u32[]{:S(2)}) collective-permute-start(bf16[4,128,256]{2,1,0:T(8,128)(2,1)S(1)} %shard_map.136.refs_1_), channel_id=1, source_target_pairs={{0,16},{16,32},{32,48},{48,64},{64,80},{80,96},{96,112},{1,17},{17... | collective-permute-start | bytes 786440 | tf_op jit(solution)/shard_map/ppermute | solution.py:28
  36.0 15.6 %copy-start.6 = (f32[256]{0:T(256)S(1)}, f32[256]{0:T(256)}, u32[]{:S(2)}) copy-start(f32[256]{0:T(256)} %param.18) | copy-start | bytes 3076
  36.0 15.5 %copy-start.7 = (f32[128]{0:T(128)S(1)}, f32[128]{0:T(128)}, u32[]{:S(2)}) copy-start(f32[128]{0:T(128)} %param.20) | copy-start | bytes 1540
  39.6 6.8 %collective-permute-start.9 = (bf16[3,128,256]{2,1,0:T(8,128)(2,1)S(1)}, bf16[3,128,256]{2,1,0:T(8,128)(2,1)S(1)}, u32[]{:S(2)}, u32[]{:S(2)}) collective-permute-start(bf16[3,128,256]{2,1,0:T(8,128)(2,1)S(1)} %pad_maximum_fusion.4), channel_id=1, source_target_pairs={{0,1},{1,2},{2,3},{3,4},{4,5},{5,6},{6,7},{7,8},{8,9},{9,10},{10,1... | collective-permute-start | bytes 589832 | tf_op jit(solution)/shard_map/ppermute | solution.py:28
  41.6 9.9 %collective-permute-start.10 = (bf16[3,128,256]{2,1,0:T(8,128)(2,1)S(1)}, bf16[3,128,256]{2,1,0:T(8,128)(2,1)S(1)}, u32[]{:S(2)}, u32[]{:S(2)}) collective-permute-start(bf16[3,128,256]{2,1,0:T(8,128)(2,1)S(1)} %pad_maximum_fusion.5), channel_id=1, source_target_pairs={{1,0},{2,1},{3,2},{4,3},{5,4},{6,5},{7,6},{8,7},{9,8},{10,9},{11,1... | collective-permute-start | bytes 589832 | tf_op jit(solution)/shard_map/ppermute | solution.py:28
  44.5 47.1 %collective-permute-start.4 = (bf16[8,144,272]{2,1,0:T(8,128)(2,1)S(1)}, bf16[8,144,272]{2,1,0:T(8,128)(2,1)S(1)}, u32[]{:S(2)}, u32[]{:S(2)}) collective-permute-start(bf16[8,144,272]{2,1,0:T(8,128)(2,1)S(1)} %constant_dynamic-update-slice_fusion.refs_0_.refs_1_), channel_id=1, source_target_pairs={{0,2},{1,3},{2,0},{3,1},{4,6},{5,7},{6,4},{7,5},{8,10},{9,11},{10,... | collective-permute-start | bytes 1880072 | tf_op jit(solution)/shard_map/ppermute | solution.py:42
  55.8 19.2 %all-to-all-start = ((bf16[16,144,128]{2,1,0:T(8,128)(2,1)}), bf16[16,144,128]{2,1,0:T(8,128)(2,1)S(1)}, u32[]{:S(2)}, u32[]{:S(2)}) async-start(bf16[16,144,128]{2,1,0:T(8,128)(2,1)} %shard_map.137), calls=%async_computation | async-start | bytes 1179648 | tf_op jit(solution)/shard_map/all_to_all | solution.py:390
  75.0 28.5 %collective-permute-start.13 = (bf16[16,144,128]{2,1,0:T(8,128)(2,1)S(1)}, bf16[16,144,128]{2,1,0:T(8,128)(2,1)S(1)}, u32[]{:S(2)}, u32[]{:S(2)}) collective-permute-start(bf16[16,144,128]{2,1,0:T(8,128)(2,1)S(1)} %all-to-all-done.refs_3_.refs_9_), channel_id=1, source_target_pairs={{0,64},{16,80},{32,96},{48,112},{64,0},{80,16},{96,32},{112,48},{1... | collective-permute-start | bytes 1769480 | tf_op jit(solution)/shard_map/ppermute | solution.py:399
  90.1 14.2 %collective-permute-start.12 = (bf16[16,144,128]{2,1,0:T(8,128)(2,1)S(1)}, bf16[16,144,128]{2,1,0:T(8,128)(2,1)S(1)}, u32[]{:S(2)}, u32[]{:S(2)}) collective-permute-start(bf16[16,144,128]{2,1,0:T(8,128)(2,1)S(1)} %all-to-all-done.refs_3_.refs_9_), channel_id=1, source_target_pairs={{0,48},{16,0},{32,16},{48,32},{64,112},{80,64},{96,80},{112,96},{1... | collective-permute-start | bytes 1769480 | tf_op jit(solution)/shard_map/ppermute | solution.py:399
  90.2 15.4 %collective-permute-start.11 = (bf16[16,144,128]{2,1,0:T(8,128)(2,1)S(1)}, bf16[16,144,128]{2,1,0:T(8,128)(2,1)S(1)}, u32[]{:S(2)}, u32[]{:S(2)}) collective-permute-start(bf16[16,144,128]{2,1,0:T(8,128)(2,1)S(1)} %all-to-all-done.refs_3_.refs_9_), channel_id=1, source_target_pairs={{0,16},{16,32},{32,48},{48,0},{64,80},{80,96},{96,112},{112,64},{1... | collective-permute-start | bytes 1769480 | tf_op jit(solution)/shard_map/ppermute | solution.py:399
  105.6 29.8 %collective-permute-start.16 = (bf16[16,144,128]{2,1,0:T(8,128)(2,1)S(1)}, bf16[16,144,128]{2,1,0:T(8,128)(2,1)S(1)}, u32[]{:S(2)}, u32[]{:S(2)}) collective-permute-start(bf16[16,144,128]{2,1,0:T(8,128)(2,1)S(1)} %collective-permute-done.11.refs_1_.refs_10_), channel_id=1, source_target_pairs={{0,64},{16,80},{32,96},{48,112},{64,0},{80,16},{96,32},{112,48},{1... | collective-permute-start | bytes 1769480 | tf_op jit(solution)/shard_map/ppermute | solution.py:399
  106.2 29.2 %collective-permute-start.15 = (bf16[16,144,128]{2,1,0:T(8,128)(2,1)S(1)}, bf16[16,144,128]{2,1,0:T(8,128)(2,1)S(1)}, u32[]{:S(2)}, u32[]{:S(2)}) collective-permute-start(bf16[16,144,128]{2,1,0:T(8,128)(2,1)S(1)} %collective-permute-done.11.refs_1_.refs_10_), channel_id=1, source_target_pairs={{0,16},{16,32},{32,48},{48,0},{64,80},{80,96},{96,112},{112,64},{1... | collective-permute-start | bytes 1769480 | tf_op jit(solution)/shard_map/ppermute | solution.py:399
  106.2 27.1 %collective-permute-start.14 = (bf16[16,144,128]{2,1,0:T(8,128)(2,1)S(1)}, bf16[16,144,128]{2,1,0:T(8,128)(2,1)S(1)}, u32[]{:S(2)}, u32[]{:S(2)}) collective-permute-start(bf16[16,144,128]{2,1,0:T(8,128)(2,1)S(1)} %all-to-all-done.refs_3_.refs_9_), channel_id=1, source_target_pairs={{0,96},{16,112},{32,64},{48,80},{64,32},{80,48},{96,0},{112,16},{1... | collective-permute-start | bytes 1769480 | tf_op jit(solution)/shard_map/ppermute | solution.py:399
  109.8 25.6 %collective-permute-start.17 = (bf16[16,144,128]{2,1,0:T(8,128)(2,1)S(1)}, bf16[16,144,128]{2,1,0:T(8,128)(2,1)S(1)}, u32[]{:S(2)}, u32[]{:S(2)}) collective-permute-start(bf16[16,144,128]{2,1,0:T(8,128)(2,1)S(1)} %collective-permute-done.13.refs_3_.refs_12_), channel_id=1, source_target_pairs={{0,48},{16,0},{32,16},{48,32},{64,112},{80,64},{96,80},{112,96},{1... | collective-permute-start | bytes 1769480 | tf_op jit(solution)/shard_map/ppermute | solution.py:399
  166.6 4.0 %collective-permute-start.18 = (f32[128,128]{1,0:T(8,128)S(1)}, f32[128,128]{1,0:T(8,128)S(1)}, u32[]{:S(2)}, u32[]{:S(2)}) collective-permute-start(f32[128,128]{1,0:T(8,128)S(1)} %get-tuple-element.36), channel_id=1, source_target_pairs={{0,1},{1,0},{2,3},{3,2},{4,5},{5,4},{6,7},{7,6},{8,9},{9,8},{10,11... | collective-permute-start | bytes 196616 | tf_op jit(solution)/shard_map/ppermute | solution.py:42
  (1 other events, 1.0 us)
where the time goes:
time: 172 us; the launch traced here: 171 us
  Pallas kernels  69 us (40%)
  starting transfers between devices  60.6 us (35%)
  waiting for transfers between devices  34.1 us (20%)
  matrix products  2.92 us (2%)
  other arithmetic  2.64 us (2%)
    pallas_call x3, Pallas kernels, attend_call(): pl.pallas_call(functools.partial(attend_kernel, len(blocks), start, finis...  62.7 us
    ppermute x8, starting transfers between devices, shifted(): lax.ppermute(x, axis, [(i, i + by) for i in range(count) if 0 <= i + by <...  23.8 us
    ppermute x7, starting transfers between devices, send(): return lax.ppermute(source, 'aa', pairs)  21.9 us
    all_to_all x1, waiting for transfers between devices, on_device(): block = lax.all_to_all(keys, 'ba', 0, 0, tiled=True)  13.4 us
    ppermute x8, waiting for transfers between devices, shifted(): lax.ppermute(x, axis, [(i, i + by) for i in range(count) if 0 <= i + by <...  13 us
    ppermute x4, starting transfers between devices, from_peer(): lax.ppermute(x, axis, [(i, i ^ bit) for i in range(lax.axis_size(axis))])  9.06 us
    ppermute x7, waiting for transfers between devices, send(): return lax.ppermute(source, 'aa', pairs)  6.87 us
    pallas_call x2, Pallas kernels, conv_call(): pl.pallas_call(kernel, in_specs=whole * (len(halo) + 1 + len(extras)), ou...  6.3 us
  transfers between devices with their start and end apart: 20, of which 12 were waited for; matrix products, arithmetic and copies ran while one was open for 3% of the time, Pallas kernels for 22%

commit v1 on v0

--- a/solution.py
+++ b/solution.py
@@ -302,7 +302,7 @@
         out_specs=out_specs,
         out_shape=out_shape,
         scratch_shapes=scratch,
-        compiler_params=pltpu.CompilerParams(vmem_limit_bytes=44 * MIB),
+        compiler_params=pltpu.CompilerParams(vmem_limit_bytes=32 * MIB),
         cost_estimate=pl.CostEstimate(
             flops=pairs * 1024, bytes_accessed=4 * MIB, transcendentals=pairs
         ),

time: 172 us -> 172 us (level)
  no operation moved by 1% of the time
where the time goes in v1:
time: 172 us; the launch traced here: 171 us
  Pallas kernels  69 us (40%)
  starting transfers between devices  60.6 us (35%)
  waiting for transfers between devices  34.1 us (20%)
  matrix products  2.92 us (2%)
  other arithmetic  2.64 us (2%)
    pallas_call x3, Pallas kernels, attend_call(): pl.pallas_call(functools.partial(attend_kernel, len(blocks), start, finis...  62.7 us
    ppermute x8, starting transfers between devices, shifted(): lax.ppermute(x, axis, [(i, i + by) for i in range(count) if 0 <= i + by <...  23.8 us
    ppermute x7, starting transfers between devices, send(): return lax.ppermute(source, 'aa', pairs)  21.9 us
    all_to_all x1, waiting for transfers between devices, on_device(): block = lax.all_to_all(keys, 'ba', 0, 0, tiled=True)  13.4 us
    ppermute x8, waiting for transfers between devices, shifted(): lax.ppermute(x, axis, [(i, i + by) for i in range(count) if 0 <= i + by <...  13 us
    ppermute x4, starting transfers between devices, from_peer(): lax.ppermute(x, axis, [(i, i ^ bit) for i in range(lax.axis_size(axis))])  9.06 us
    ppermute x7, waiting for transfers between devices, send(): return lax.ppermute(source, 'aa', pairs)  6.87 us
    pallas_call x2, Pallas kernels, conv_call(): pl.pallas_call(kernel, in_specs=whole * (len(halo) + 1 + len(extras)), ou...  6.3 us
  transfers between devices with their start and end apart: 20, of which 12 were waited for; matrix products, arithmetic and copies ran while one was open for 3% of the time, Pallas kernels for 22%

profile of v1, /device:TPU:1, one launch (start us, length us, event | category | flops | bytes accessed | tf_op | source)
XLA Modules:
  0.0 171.2 jit_solution(1941017889123635955)
XLA Ops:
  0.0 1.4 collective-permute-start.1
  1.4 5.0 %collective-permute-start = (bf16[4,128,256]{2,1,0:T(8,128)(2,1)}, bf16[4,128,256]{2,1,0:T(8,128)(2,1)S(1)}, u32[]{:S(2)}, u32[]{:S(2)}) collective-permute-start(bf16[4,128,256]{2,1,0:T(8,128)(2,1)} %bitcast.25), channel_id=1, source_target_pairs={{0,16},{16,32},{32,48},{48,64},{64,80},{80,96},{96,112},{1,17},{17... | collective-permute-start | bytes 786440 | tf_op jit(solution)/shard_map/ppermute | solution.py:28
  6.5 1.1 convert_element_type.14
  11.8 4.9 %collective-permute-start.5 = (bf16[3,128,256]{2,1,0:T(8,128)(2,1)S(1)}, bf16[3,128,256]{2,1,0:T(8,128)(2,1)S(1)}, u32[]{:S(2)}, u32[]{:S(2)}) collective-permute-start(bf16[3,128,256]{2,1,0:T(8,128)(2,1)S(1)} %pad_maximum_fusion.2), channel_id=1, source_target_pairs={{0,1},{1,2},{2,3},{3,4},{4,5},{5,6},{6,7},{7,8},{8,9},{9,10},{10,1... | collective-permute-start | bytes 589832 | tf_op jit(solution)/shard_map/ppermute | solution.py:28
  16.7 1.9 %collective-permute-start.6 = (bf16[3,128,256]{2,1,0:T(8,128)(2,1)S(1)}, bf16[3,128,256]{2,1,0:T(8,128)(2,1)S(1)}, u32[]{:S(2)}, u32[]{:S(2)}) collective-permute-start(bf16[3,128,256]{2,1,0:T(8,128)(2,1)S(1)} %pad_maximum_fusion.3), channel_id=1, source_target_pairs={{1,0},{2,1},{3,2},{4,3},{5,4},{6,5},{7,6},{8,7},{9,8},{10,9},{11,1... | collective-permute-start | bytes 589832 | tf_op jit(solution)/shard_map/ppermute | solution.py:28
  18.7 1.3 convolution_multiply_fusion.refs_9_
  20.0 1.3 collective-permute-start.2
  21.3 2.4 %collective-permute-done.6.refs_4_ = bf16[3,128,256]{2,1,0:T(8,128)(2,1)S(1)} collective-permute-done((bf16[3,128,256]{2,1,0:T(8,128)(2,1)S(1)}, bf16[3,128,256]{2,1,0:T(8,128)(2,1)S(1)}, u32[]{:S(2)}, u32[]{:S(2)}) %collective-permute-start.6) | collective-permute-done | bytes 196640 | tf_op jit(solution)/shard_map/ppermute | solution.py:28
  23.7 2.0 %shard_map.136.refs_1_ = bf16[4,128,256]{2,1,0:T(8,128)(2,1)S(1)} custom-call(bf16[4,128,256]{2,1,0:T(8,128)(2,1)S(1)} %collective-permute-done.refs_0_, bf16[4,128,256]{2,1,0:T(8,128)(2,1)S(1)} %bitcast.26, bf16[4,128,256]{2,1,0:T(8,128)(2,1)S(1)} %collective-permute-done.1.refs_2_, bf16[3,128,256]{2,1,0:T(8,128)(2,1)S(1)} %collective-permute-done.5.refs_3_, ...), custom_call_target="tpu_custom_call" | custom-call | flops 1811939328 | bytes 3538944 | tf_op jit(solution)/shard_map/pallas_call | solution.py:124
  25.8 1.3 collective-permute-start.8
  27.2 2.7 %collective-permute-start.3 = (bf16[4,144,272]{2,1,0:T(8,128)(2,1)S(1)}, bf16[4,144,272]{2,1,0:T(8,128)(2,1)S(1)}, u32[]{:S(2)}, u32[]{:S(2)}) collective-permute-start(bf16[4,144,272]{2,1,0:T(8,128)(2,1)S(1)} %pad_maximum_fusion), channel_id=1, source_target_pairs={{0,4},{1,5},{2,6},{3,7},{4,0},{5,1},{6,2},{7,3},{8,12},{9,13},{10,... | collective-permute-start | bytes 940040 | tf_op jit(solution)/shard_map/ppermute | solution.py:42
  29.9 4.6 %collective-permute-start.7 = (bf16[4,128,256]{2,1,0:T(8,128)(2,1)S(1)}, bf16[4,128,256]{2,1,0:T(8,128)(2,1)S(1)}, u32[]{:S(2)}, u32[]{:S(2)}) collective-permute-start(bf16[4,128,256]{2,1,0:T(8,128)(2,1)S(1)} %shard_map.136.refs_1_), channel_id=1, source_target_pairs={{0,16},{16,32},{32,48},{48,64},{64,80},{80,96},{96,112},{1,17},{17... | collective-permute-start | bytes 786440 | tf_op jit(solution)/shard_map/ppermute | solution.py:28
  34.6 1.4 collective-permute-done.8.refs_2_
  36.0 3.6 %collective-permute-done.7.refs_0_ = bf16[4,128,256]{2,1,0:T(8,128)(2,1)S(1)} collective-permute-done((bf16[4,128,256]{2,1,0:T(8,128)(2,1)S(1)}, bf16[4,128,256]{2,1,0:T(8,128)(2,1)S(1)}, u32[]{:S(2)}, u32[]{:S(2)}) %collective-permute-start.7) | collective-permute-done | bytes 262176 | tf_op jit(solution)/shard_map/ppermute | solution.py:28
  39.6 1.9 %collective-permute-start.9 = (bf16[3,128,256]{2,1,0:T(8,128)(2,1)S(1)}, bf16[3,128,256]{2,1,0:T(8,128)(2,1)S(1)}, u32[]{:S(2)}, u32[]{:S(2)}) collective-permute-start(bf16[3,128,256]{2,1,0:T(8,128)(2,1)S(1)} %pad_maximum_fusion.4), channel_id=1, source_target_pairs={{0,1},{1,2},{2,3},{3,4},{4,5},{5,6},{6,7},{7,8},{8,9},{9,10},{10,1... | collective-permute-start | bytes 589832 | tf_op jit(solution)/shard_map/ppermute | solution.py:28
  41.6 2.7 %collective-permute-start.10 = (bf16[3,128,256]{2,1,0:T(8,128)(2,1)S(1)}, bf16[3,128,256]{2,1,0:T(8,128)(2,1)S(1)}, u32[]{:S(2)}, u32[]{:S(2)}) collective-permute-start(bf16[3,128,256]{2,1,0:T(8,128)(2,1)S(1)} %pad_maximum_fusion.5), channel_id=1, source_target_pairs={{1,0},{2,1},{3,2},{4,3},{5,4},{6,5},{7,6},{8,7},{9,8},{10,9},{11,1... | collective-permute-start | bytes 589832 | tf_op jit(solution)/shard_map/ppermute | solution.py:28
  44.5 2.0 %collective-permute-start.4 = (bf16[8,144,272]{2,1,0:T(8,128)(2,1)S(1)}, bf16[8,144,272]{2,1,0:T(8,128)(2,1)S(1)}, u32[]{:S(2)}, u32[]{:S(2)}) collective-permute-start(bf16[8,144,272]{2,1,0:T(8,128)(2,1)S(1)} %constant_dynamic-update-slice_fusion.refs_0_.refs_1_), channel_id=1, source_target_pairs={{0,2},{1,3},{2,0},{3,1},{4,6},{5,7},{6,4},{7,5},{8,10},{9,11},{10,... | collective-permute-start | bytes 1880072 | tf_op jit(solution)/shard_map/ppermute | solution.py:42
  46.4 5.1 %collective-permute-done.10.refs_4_ = bf16[3,128,256]{2,1,0:T(8,128)(2,1)S(1)} collective-permute-done((bf16[3,128,256]{2,1,0:T(8,128)(2,1)S(1)}, bf16[3,128,256]{2,1,0:T(8,128)(2,1)S(1)}, u32[]{:S(2)}, u32[]{:S(2)}) %collective-permute-start.10) | collective-permute-done | bytes 196640 | tf_op jit(solution)/shard_map/ppermute | solution.py:28
  51.5 4.3 %shard_map.137 = bf16[16,144,128]{2,1,0:T(8,128)(2,1)} custom-call(bf16[4,128,256]{2,1,0:T(8,128)(2,1)S(1)} %collective-permute-done.7.refs_0_, bf16[4,128,256]{2,1,0:T(8,128)(2,1)S(1)} %shard_map.136.refs_1_, bf16[4,128,256]{2,1,0:T(8,128)(2,1)S(1)} %collective-permute-done.8.refs_2_, bf16[3,128,256]{2,1,0:T(8,128)(2,1)S(1)} %collective-permute-done.9.refs_3_, ...), custom_call_target="tpu_custom_call" | custom-call | flops 1811939328 | bytes 3538944 | tf_op jit(solution)/shard_map/pallas_call | solution.py:124
  55.8 5.8 %all-to-all-start = ((bf16[16,144,128]{2,1,0:T(8,128)(2,1)}), bf16[16,144,128]{2,1,0:T(8,128)(2,1)S(1)}, u32[]{:S(2)}, u32[]{:S(2)}) async-start(bf16[16,144,128]{2,1,0:T(8,128)(2,1)} %shard_map.137), calls=%async_computation | async-start | bytes 1179648 | tf_op jit(solution)/shard_map/all_to_all | solution.py:390
  61.6 13.4 %all-to-all-done.refs_3_.refs_9_ = bf16[16,144,128]{2,1,0:T(8,128)(2,1)S(1)} async-done(((bf16[16,144,128]{2,1,0:T(8,128)(2,1)}), bf16[16,144,128]{2,1,0:T(8,128)(2,1)S(1)}, u32[]{:S(2)}, u32[]{:S(2)}) %all-to-all-start) | async-done | bytes 589856 | tf_op jit(solution)/shard_map/all_to_all | solution.py:390
  75.0 15.1 %collective-permute-start.13 = (bf16[16,144,128]{2,1,0:T(8,128)(2,1)S(1)}, bf16[16,144,128]{2,1,0:T(8,128)(2,1)S(1)}, u32[]{:S(2)}, u32[]{:S(2)}) collective-permute-start(bf16[16,144,128]{2,1,0:T(8,128)(2,1)S(1)} %all-to-all-done.refs_3_.refs_9_), channel_id=1, source_target_pairs={{0,64},{16,80},{32,96},{48,112},{64,0},{80,16},{96,32},{112,48},{1... | collective-permute-start | bytes 1769480 | tf_op jit(solution)/shard_map/ppermute | solution.py:399
  90.2 1.5 collective-permute-start.11
  91.6 9.6 %shard_map.138 = (bf16[32,144,128]{2,1,0:T(8,128)(2,1)S(1)}, f32[1,4096]{1,0:T(1,128)S(1)}, f32[32,144,128]{2,1,0:T(8,128)S(1)}) custom-call(bf16[8,144,272]{2,1,0:T(8,128)(2,1)S(1)} %constant_dynamic-update-slice_fusion.refs_0_.refs_1_, bf16[8,144,272]{2,1,0:T(8,128)(2,1)S(1)} %collective-permute-done.4.refs_1_.refs_2_, s32[2]{0:T(128)S(1)} %pad_add_fusion.refs_2_, ...), custom_call_target="tpu_custom_call" | custom-call | flops 8589934592 | bytes 4194304 | tf_op jit(solution)/shard_map/pallas_call | solution.py:298
  101.2 2.3 %collective-permute-done.13.refs_3_.refs_12_ = bf16[16,144,128]{2,1,0:T(8,128)(2,1)S(1)} collective-permute-done((bf16[16,144,128]{2,1,0:T(8,128)(2,1)S(1)}, bf16[16,144,128]{2,1,0:T(8,128)(2,1)S(1)}, u32[]{:S(2)}, u32[]{:S(2)}) %collective-permute-start.13) | collective-permute-done | bytes 589856 | tf_op jit(solution)/shard_map/ppermute | solution.py:399
  104.3 1.2 collective-permute-done.11.refs_1_.refs_10_
  106.2 3.6 %collective-permute-start.14 = (bf16[16,144,128]{2,1,0:T(8,128)(2,1)S(1)}, bf16[16,144,128]{2,1,0:T(8,128)(2,1)S(1)}, u32[]{:S(2)}, u32[]{:S(2)}) collective-permute-start(bf16[16,144,128]{2,1,0:T(8,128)(2,1)S(1)} %all-to-all-done.refs_3_.refs_9_), channel_id=1, source_target_pairs={{0,96},{16,112},{32,64},{48,80},{64,32},{80,48},{96,0},{112,16},{1... | collective-permute-start | bytes 1769480 | tf_op jit(solution)/shard_map/ppermute | solution.py:399
  109.8 1.1 collective-permute-start.17
  110.9 22.0 %shard_map.139 = (f32[1,4096]{1,0:T(1,128)S(1)}, f32[32,144,128]{2,1,0:T(8,128)S(1)}) custom-call(bf16[32,144,128]{2,1,0:T(8,128)(2,1)S(1)} %get-tuple-element.24.refs_0_, bf16[16,144,128]{2,1,0:T(8,128)(2,1)S(1)} %collective-permute-done.11.refs_1_.refs_10_, bf16[16,144,128]{2,1,0:T(8,128)(2,1)S(1)} %collective-permute-done.12.refs_2_.refs_11_, ...), custom_call_target="tpu_custom_call" | custom-call | flops 25769803776 | bytes 4194304 | tf_op jit(solution)/shard_map/pallas_call | solution.py:298
  133.3 2.1 %collective-permute-done.17.refs_6_ = bf16[16,144,128]{2,1,0:T(8,128)(2,1)S(1)} collective-permute-done((bf16[16,144,128]{2,1,0:T(8,128)(2,1)S(1)}, bf16[16,144,128]{2,1,0:T(8,128)(2,1)S(1)}, u32[]{:S(2)}, u32[]{:S(2)}) %collective-permute-start.17) | collective-permute-done | bytes 589856 | tf_op jit(solution)/shard_map/ppermute | solution.py:399
  135.4 31.2 %shard_map.140 = (f32[128,128]{1,0:T(8,128)S(1)}, f32[128,128]{1,0:T(8,128)S(1)}) custom-call(bf16[32,144,128]{2,1,0:T(8,128)(2,1)S(1)} %get-tuple-element.24.refs_0_, bf16[8,144,272]{2,1,0:T(8,128)(2,1)S(1)} %constant_dynamic-update-slice_fusion.refs_0_.refs_1_, bf16[8,144,272]{2,1,0:T(8,128)(2,1)S(1)} %collective-permute-done.4.refs_1_.refs_2_, ...), custom_call_target="tpu_custom_call" | custom-call | flops 34359738368 | bytes 4194304 | tf_op jit(solution)/shard_map/pallas_call | solution.py:298
  166.6 3.1 %collective-permute-start.18 = (f32[128,128]{1,0:T(8,128)S(1)}, f32[128,128]{1,0:T(8,128)S(1)}, u32[]{:S(2)}, u32[]{:S(2)}) collective-permute-start(f32[128,128]{1,0:T(8,128)S(1)} %get-tuple-element.36), channel_id=1, source_target_pairs={{0,1},{1,0},{2,3},{3,2},{4,5},{5,4},{6,7},{7,6},{8,9},{9,8},{10,11... | collective-permute-start | bytes 196616 | tf_op jit(solution)/shard_map/ppermute | solution.py:42
  (67 shorter events, 7.8 us)
Async XLA Ops:
  0.0 10.8 %copy-start = (bf16[128,128]{1,0:T(8,128)(2,1)S(1)}, bf16[128,128]{1,0:T(8,128)(2,1)}, u32[]{:S(2)}) copy-start(bf16[128,128]{1,0:T(8,128)(2,1)} %param.27) | copy-start | bytes 98308
  0.0 7.7 %copy-start.8 = (f32[2048]{0:T(1024)S(1)}, f32[2048]{0:T(1024)}, u32[]{:S(2)}) copy-start(f32[2048]{0:T(1024)} %param.22) | copy-start | bytes 24580
  0.0 8.0 %copy-start.9 = (f32[2048]{0:T(1024)S(1)}, f32[2048]{0:T(1024)}, u32[]{:S(2)}) copy-start(f32[2048]{0:T(1024)} %param.23) | copy-start | bytes 24580
  0.0 11.2 %collective-permute-start.1 = (bf16[4,128,256]{2,1,0:T(8,128)(2,1)}, bf16[4,128,256]{2,1,0:T(8,128)(2,1)S(1)}, u32[]{:S(2)}, u32[]{:S(2)}) collective-permute-start(bf16[4,128,256]{2,1,0:T(8,128)(2,1)} %bitcast.24), channel_id=1, source_target_pairs={{16,0},{32,16},{48,32},{64,48},{80,64},{96,80},{112,96},{17,1},{33... | collective-permute-start | bytes 786440 | tf_op jit(solution)/shard_map/ppermute | solution.py:28
  1.4 10.3 %collective-permute-start = (bf16[4,128,256]{2,1,0:T(8,128)(2,1)}, bf16[4,128,256]{2,1,0:T(8,128)(2,1)S(1)}, u32[]{:S(2)}, u32[]{:S(2)}) collective-permute-start(bf16[4,128,256]{2,1,0:T(8,128)(2,1)} %bitcast.25), channel_id=1, source_target_pairs={{0,16},{16,32},{32,48},{48,64},{64,80},{80,96},{96,112},{1,17},{17... | collective-permute-start | bytes 786440 | tf_op jit(solution)/shard_map/ppermute | solution.py:28
  7.9 1.2 copy-start.11
  8.0 1.3 copy-start.12
  10.1 1.1 copy-start.1
  11.7 12.0 %copy-start.2 = (bf16[3,3,3,256,256]{4,3,2,1,0:T(8,128)(2,1)S(1)}, bf16[3,3,3,256,256]{4,3,2,1,0:T(8,128)(2,1)}, u32[]{:S(2)}) copy-start(bf16[3,3,3,256,256]{4,3,2,1,0:T(8,128)(2,1)} %refs_5_.2) | copy-start | bytes 10616836
  11.8 9.5 %collective-permute-start.5 = (bf16[3,128,256]{2,1,0:T(8,128)(2,1)S(1)}, bf16[3,128,256]{2,1,0:T(8,128)(2,1)S(1)}, u32[]{:S(2)}, u32[]{:S(2)}) collective-permute-start(bf16[3,128,256]{2,1,0:T(8,128)(2,1)S(1)} %pad_maximum_fusion.2), channel_id=1, source_target_pairs={{0,1},{1,2},{2,3},{3,4},{4,5},{5,6},{6,7},{7,8},{8,9},{9,10},{10,1... | collective-permute-start | bytes 589832 | tf_op jit(solution)/shard_map/ppermute | solution.py:28
  16.7 7.0 %copy-start.5 = (f32[256]{0:T(256)S(1)}, f32[256]{0:T(256)}, u32[]{:S(2)}) copy-start(f32[256]{0:T(256)} %param.16) | copy-start | bytes 3076
  16.7 7.0 %collective-permute-start.6 = (bf16[3,128,256]{2,1,0:T(8,128)(2,1)S(1)}, bf16[3,128,256]{2,1,0:T(8,128)(2,1)S(1)}, u32[]{:S(2)}, u32[]{:S(2)}) collective-permute-start(bf16[3,128,256]{2,1,0:T(8,128)(2,1)S(1)} %pad_maximum_fusion.3), channel_id=1, source_target_pairs={{1,0},{2,1},{3,2},{4,3},{5,4},{6,5},{7,6},{8,7},{9,8},{10,9},{11,1... | collective-permute-start | bytes 589832 | tf_op jit(solution)/shard_map/ppermute | solution.py:28
  20.0 7.1 %collective-permute-start.2 = (bf16[2,144,272]{2,1,0:T(8,128)(2,1)S(1)}, bf16[2,144,272]{2,1,0:T(8,128)(2,1)S(1)}, u32[]{:S(2)}, u32[]{:S(2)}) collective-permute-start(bf16[2,144,272]{2,1,0:T(8,128)(2,1)S(1)} %pad_maximum_fusion.1), channel_id=1, source_target_pairs={{0,8},{1,9},{2,10},{3,11},{4,12},{5,13},{6,14},{7,15},{8,0},{9,1},... | collective-permute-start | bytes 470024 | tf_op jit(solution)/shard_map/ppermute | solution.py:42
  23.7 27.8 %copy-start.4 = (bf16[2,2,256,128]{3,2,1,0:T(8,128)(2,1)S(1)}, bf16[2,2,256,128]{3,2,1,0:T(8,128)(2,1)}, u32[]{:S(2)}) copy-start(bf16[2,2,256,128]{3,2,1,0:T(8,128)(2,1)} %refs_7_.1) | copy-start | bytes 786436
  25.8 10.2 %collective-permute-start.8 = (bf16[4,128,256]{2,1,0:T(8,128)(2,1)S(1)}, bf16[4,128,256]{2,1,0:T(8,128)(2,1)S(1)}, u32[]{:S(2)}, u32[]{:S(2)}) collective-permute-start(bf16[4,128,256]{2,1,0:T(8,128)(2,1)S(1)} %shard_map.136.refs_1_), channel_id=1, source_target_pairs={{16,0},{32,16},{48,32},{64,48},{80,64},{96,80},{112,96},{17,1},{33... | collective-permute-start | bytes 786440 | tf_op jit(solution)/shard_map/ppermute | solution.py:28
  27.1 24.4 %copy-start.3 = (bf16[3,3,3,256,256]{4,3,2,1,0:T(8,128)(2,1)S(1)}, bf16[3,3,3,256,256]{4,3,2,1,0:T(8,128)(2,1)}, u32[]{:S(2)}) copy-start(bf16[3,3,3,256,256]{4,3,2,1,0:T(8,128)(2,1)} %refs_5_.3) | copy-start | bytes 10616836
  27.2 17.2 %collective-permute-start.3 = (bf16[4,144,272]{2,1,0:T(8,128)(2,1)S(1)}, bf16[4,144,272]{2,1,0:T(8,128)(2,1)S(1)}, u32[]{:S(2)}, u32[]{:S(2)}) collective-permute-start(bf16[4,144,272]{2,1,0:T(8,128)(2,1)S(1)} %pad_maximum_fusion), channel_id=1, source_target_pairs={{0,4},{1,5},{2,6},{3,7},{4,0},{5,1},{6,2},{7,3},{8,12},{9,13},{10,... | collective-permute-start | bytes 940040 | tf_op jit(solution)/shard_map/ppermute | solution.py:42
  29.9 9.7 %collective-permute-start.7 = (bf16[4,128,256]{2,1,0:T(8,128)(2,1)S(1)}, bf16[4,128,256]{2,1,0:T(8,128)(2,1)S(1)}, u32[]{:S(2)}, u32[]{:S(2)}) collective-permute-start(bf16[4,128,256]{2,1,0:T(8,128)(2,1)S(1)} %shard_map.136.refs_1_), channel_id=1, source_target_pairs={{0,16},{16,32},{32,48},{48,64},{64,80},{80,96},{96,112},{1,17},{17... | collective-permute-start | bytes 786440 | tf_op jit(solution)/shard_map/ppermute | solution.py:28
  36.0 15.6 %copy-start.6 = (f32[256]{0:T(256)S(1)}, f32[256]{0:T(256)}, u32[]{:S(2)}) copy-start(f32[256]{0:T(256)} %param.18) | copy-start | bytes 3076
  36.0 15.5 %copy-start.7 = (f32[128]{0:T(128)S(1)}, f32[128]{0:T(128)}, u32[]{:S(2)}) copy-start(f32[128]{0:T(128)} %param.20) | copy-start | bytes 1540
  39.6 6.8 %collective-permute-start.9 = (bf16[3,128,256]{2,1,0:T(8,128)(2,1)S(1)}, bf16[3,128,256]{2,1,0:T(8,128)(2,1)S(1)}, u32[]{:S(2)}, u32[]{:S(2)}) collective-permute-start(bf16[3,128,256]{2,1,0:T(8,128)(2,1)S(1)} %pad_maximum_fusion.4), channel_id=1, source_target_pairs={{0,1},{1,2},{2,3},{3,4},{4,5},{5,6},{6,7},{7,8},{8,9},{9,10},{10,1... | collective-permute-start | bytes 589832 | tf_op jit(solution)/shard_map/ppermute | solution.py:28
  41.6 9.9 %collective-permute-start.10 = (bf16[3,128,256]{2,1,0:T(8,128)(2,1)S(1)}, bf16[3,128,256]{2,1,0:T(8,128)(2,1)S(1)}, u32[]{:S(2)}, u32[]{:S(2)}) collective-permute-start(bf16[3,128,256]{2,1,0:T(8,128)(2,1)S(1)} %pad_maximum_fusion.5), channel_id=1, source_target_pairs={{1,0},{2,1},{3,2},{4,3},{5,4},{6,5},{7,6},{8,7},{9,8},{10,9},{11,1... | collective-permute-start | bytes 589832 | tf_op jit(solution)/shard_map/ppermute | solution.py:28
  44.5 47.1 %collective-permute-start.4 = (bf16[8,144,272]{2,1,0:T(8,128)(2,1)S(1)}, bf16[8,144,272]{2,1,0:T(8,128)(2,1)S(1)}, u32[]{:S(2)}, u32[]{:S(2)}) collective-permute-start(bf16[8,144,272]{2,1,0:T(8,128)(2,1)S(1)} %constant_dynamic-update-slice_fusion.refs_0_.refs_1_), channel_id=1, source_target_pairs={{0,2},{1,3},{2,0},{3,1},{4,6},{5,7},{6,4},{7,5},{8,10},{9,11},{10,... | collective-permute-start | bytes 1880072 | tf_op jit(solution)/shard_map/ppermute | solution.py:42
  55.8 19.2 %all-to-all-start = ((bf16[16,144,128]{2,1,0:T(8,128)(2,1)}), bf16[16,144,128]{2,1,0:T(8,128)(2,1)S(1)}, u32[]{:S(2)}, u32[]{:S(2)}) async-start(bf16[16,144,128]{2,1,0:T(8,128)(2,1)} %shard_map.137), calls=%async_computation | async-start | bytes 1179648 | tf_op jit(solution)/shard_map/all_to_all | solution.py:390
  75.0 28.5 %collective-permute-start.13 = (bf16[16,144,128]{2,1,0:T(8,128)(2,1)S(1)}, bf16[16,144,128]{2,1,0:T(8,128)(2,1)S(1)}, u32[]{:S(2)}, u32[]{:S(2)}) collective-permute-start(bf16[16,144,128]{2,1,0:T(8,128)(2,1)S(1)} %all-to-all-done.refs_3_.refs_9_), channel_id=1, source_target_pairs={{0,64},{16,80},{32,96},{48,112},{64,0},{80,16},{96,32},{112,48},{1... | collective-permute-start | bytes 1769480 | tf_op jit(solution)/shard_map/ppermute | solution.py:399
  90.1 14.2 %collective-permute-start.12 = (bf16[16,144,128]{2,1,0:T(8,128)(2,1)S(1)}, bf16[16,144,128]{2,1,0:T(8,128)(2,1)S(1)}, u32[]{:S(2)}, u32[]{:S(2)}) collective-permute-start(bf16[16,144,128]{2,1,0:T(8,128)(2,1)S(1)} %all-to-all-done.refs_3_.refs_9_), channel_id=1, source_target_pairs={{0,48},{16,0},{32,16},{48,32},{64,112},{80,64},{96,80},{112,96},{1... | collective-permute-start | bytes 1769480 | tf_op jit(solution)/shard_map/ppermute | solution.py:399
  90.2 15.4 %collective-permute-start.11 = (bf16[16,144,128]{2,1,0:T(8,128)(2,1)S(1)}, bf16[16,144,128]{2,1,0:T(8,128)(2,1)S(1)}, u32[]{:S(2)}, u32[]{:S(2)}) collective-permute-start(bf16[16,144,128]{2,1,0:T(8,128)(2,1)S(1)} %all-to-all-done.refs_3_.refs_9_), channel_id=1, source_target_pairs={{0,16},{16,32},{32,48},{48,0},{64,80},{80,96},{96,112},{112,64},{1... | collective-permute-start | bytes 1769480 | tf_op jit(solution)/shard_map/ppermute | solution.py:399
  105.6 29.8 %collective-permute-start.16 = (bf16[16,144,128]{2,1,0:T(8,128)(2,1)S(1)}, bf16[16,144,128]{2,1,0:T(8,128)(2,1)S(1)}, u32[]{:S(2)}, u32[]{:S(2)}) collective-permute-start(bf16[16,144,128]{2,1,0:T(8,128)(2,1)S(1)} %collective-permute-done.11.refs_1_.refs_10_), channel_id=1, source_target_pairs={{0,64},{16,80},{32,96},{48,112},{64,0},{80,16},{96,32},{112,48},{1... | collective-permute-start | bytes 1769480 | tf_op jit(solution)/shard_map/ppermute | solution.py:399
  106.2 29.2 %collective-permute-start.15 = (bf16[16,144,128]{2,1,0:T(8,128)(2,1)S(1)}, bf16[16,144,128]{2,1,0:T(8,128)(2,1)S(1)}, u32[]{:S(2)}, u32[]{:S(2)}) collective-permute-start(bf16[16,144,128]{2,1,0:T(8,128)(2,1)S(1)} %collective-permute-done.11.refs_1_.refs_10_), channel_id=1, source_target_pairs={{0,16},{16,32},{32,48},{48,0},{64,80},{80,96},{96,112},{112,64},{1... | collective-permute-start | bytes 1769480 | tf_op jit(solution)/shard_map/ppermute | solution.py:399
  106.2 27.1 %collective-permute-start.14 = (bf16[16,144,128]{2,1,0:T(8,128)(2,1)S(1)}, bf16[16,144,128]{2,1,0:T(8,128)(2,1)S(1)}, u32[]{:S(2)}, u32[]{:S(2)}) collective-permute-start(bf16[16,144,128]{2,1,0:T(8,128)(2,1)S(1)} %all-to-all-done.refs_3_.refs_9_), channel_id=1, source_target_pairs={{0,96},{16,112},{32,64},{48,80},{64,32},{80,48},{96,0},{112,16},{1... | collective-permute-start | bytes 1769480 | tf_op jit(solution)/shard_map/ppermute | solution.py:399
  109.8 25.6 %collective-permute-start.17 = (bf16[16,144,128]{2,1,0:T(8,128)(2,1)S(1)}, bf16[16,144,128]{2,1,0:T(8,128)(2,1)S(1)}, u32[]{:S(2)}, u32[]{:S(2)}) collective-permute-start(bf16[16,144,128]{2,1,0:T(8,128)(2,1)S(1)} %collective-permute-done.13.refs_3_.refs_12_), channel_id=1, source_target_pairs={{0,48},{16,0},{32,16},{48,32},{64,112},{80,64},{96,80},{112,96},{1... | collective-permute-start | bytes 1769480 | tf_op jit(solution)/shard_map/ppermute | solution.py:399
  166.6 4.0 %collective-permute-start.18 = (f32[128,128]{1,0:T(8,128)S(1)}, f32[128,128]{1,0:T(8,128)S(1)}, u32[]{:S(2)}, u32[]{:S(2)}) collective-permute-start(f32[128,128]{1,0:T(8,128)S(1)} %get-tuple-element.36), channel_id=1, source_target_pairs={{0,1},{1,0},{2,3},{3,2},{4,5},{5,4},{6,7},{7,6},{8,9},{9,8},{10,11... | collective-permute-start | bytes 196616 | tf_op jit(solution)/shard_map/ppermute | solution.py:42
  (1 other events, 1.0 us)
